TPU v7x, 1024 devices: a whole 4x4x32 slice. The times are simulated.
1024 devices in a mesh: rep: 64 (over z_hi, x, y), fsdp: 16 (over z_lo, core).
Axes of the slice: x: 4, y: 4, z: 32 (z_hi: 4, z_lo: 8; z = z_hi * 8 + z_lo), core: 2. Of those that a mesh axis runs over, the one named last changes fastest.
Arguments:
- grad_partial: bfloat16 [64, 64, 512, 512], P('rep', 'fsdp'), may hold values from -2 to 2
- owner_block: int32 [64], replicated, may hold values from 0 to 63, each once
- left_stat: float32 [64, 512, 512], P('rep', 'fsdp'), may hold values from -0.1 to 1.6, as said below
- right_stat: float32 [64, 512, 512], P('rep'), may hold values from -0.1 to 1.6, as said below
- left_root: float32 [64, 512, 512], P('rep'), may hold values from -0.05 to 1, as said below
- right_root: float32 [64, 512, 512], P('rep'), may hold values from -0.05 to 1, as said below
Outputs:
- preconditioned: bfloat16 [64, 512, 512], P('rep', 'fsdp')
- left_new: float32 [64, 512, 512], P('rep', 'fsdp')
- right_new: float32 [64, 512, 512], P('rep', 'fsdp')
- left_next: float32 [64, 512, 512], P('rep', 'fsdp')
- right_next: float32 [64, 512, 512], P('rep', 'fsdp')
Inputs may be any that keep to these rules, and one draw needn't show every extreme that they name: `owner_block`: every block number appears exactly once. `left_stat`: each slot's matrix is symmetric positive definite. `right_stat`: each slot's matrix is symmetric positive definite. `left_root`: each slot's matrix is symmetric. `right_root`: each slot's matrix is symmetric.
All inputs are finite; a program needn't handle non-finite values.
Results may differ from a plain program's by a relative error of at most 0.0068.
Values may be sent and summed in bfloat16 or wider, within the bound.
No kernel may reach another device: no remote copies, remote signals or barrier semaphores. Data moves between devices by JAX's collectives and lax.ppermute only.
A program may use at most 32 MiB of HBM per device.

v0:
```python
import jax
import jax.numpy as jnp
from jax import lax
from jax.sharding import PartitionSpec as P

decay_rate = 0.9


def newton_step(stat_rows, root_full, root_rows):
    product = stat_rows
    for power in range(5):
        product = jnp.dot(
            product, root_full, precision=lax.Precision.HIGHEST, preferred_element_type=jnp.float32
        )
    return (5.0 * root_rows - product) / 4.0


def per_device(grad_partial, owner_block, left_stat, right_stat, left_root, right_root):
    block_size = grad_partial.shape[-1]
    gram_weight = (1.0 - decay_rate) / block_size
    local_blocks = grad_partial.reshape(grad_partial.shape[1], block_size, block_size)
    regrouped = lax.all_to_all(local_blocks, "fsdp", split_axis=1, concat_axis=0, tiled=True)
    slab_rows = regrouped.shape[1]
    selected = jnp.take(regrouped, owner_block, axis=0).astype(jnp.float32)
    summed = lax.psum_scatter(selected, "rep", scatter_dimension=0, tiled=True)
    grad_slab = summed[0].astype(jnp.bfloat16)
    full_block = lax.all_gather(grad_slab, "fsdp", axis=0, tiled=True)
    row_start = lax.axis_index("fsdp") * slab_rows
    left_old = left_stat[0]
    right_old = right_stat[0]
    left_guess = left_root[0]
    right_guess = right_root[0]
    left_upd = decay_rate * left_old + gram_weight * lax.dot_general(
        grad_slab, full_block, (((1,), (1,)), ((), ())), preferred_element_type=jnp.float32
    )
    left_rows = lax.dynamic_slice_in_dim(left_guess, row_start, slab_rows, 0)
    left_ref = newton_step(left_upd, left_guess, left_rows)
    right_full = decay_rate * right_old + gram_weight * lax.dot_general(
        full_block, full_block, (((0,), (0,)), ((), ())), preferred_element_type=jnp.float32
    )
    right_ref_full = newton_step(right_full, right_guess, right_guess)
    right_upd = lax.dynamic_slice_in_dim(right_full, row_start, slab_rows, 0)
    right_ref = lax.dynamic_slice_in_dim(right_ref_full, row_start, slab_rows, 0)
    right_cast = right_ref_full.astype(jnp.bfloat16)
    left_half = jnp.dot(
        left_ref.astype(jnp.bfloat16), full_block, preferred_element_type=jnp.float32
    ).astype(jnp.bfloat16)
    result = jnp.dot(left_half, right_cast, preferred_element_type=jnp.float32).astype(jnp.bfloat16)
    return (result[None], left_upd[None], right_upd[None], left_ref[None], right_ref[None])


def solution(mesh):
    in_specs = (
        P("rep", "fsdp", None, None),
        P(),
        P("rep", "fsdp", None),
        P("rep", None, None),
        P("rep", None, None),
        P("rep", None, None),
    )
    out_specs = (
        P("rep", "fsdp", None),
        P("rep", "fsdp", None),
        P("rep", "fsdp", None),
        P("rep", "fsdp", None),
        P("rep", "fsdp", None),
    )
    return jax.shard_map(
        per_device, mesh=mesh, in_specs=in_specs, out_specs=out_specs, check_vma=False
    )
```

profile of v0, /device:TPU:1, one launch (start us, length us, event | category | flops | bytes accessed | tf_op | source)
XLA Modules:
  0.0 821.3 jit_solution(14997316173274601929)
XLA Ops:
  7.2 4.5 copy.16
  11.7 17.8 %all-to-all-start = ((bf16[4,512,512]{2,0,1:T(4,128)(2,1)}), bf16[4,512,512]{2,0,1:T(4,128)(2,1)S(1)}, u32[]{:S(2)}, u32[]{:S(2)}) async-start(bf16[4,512,512]{2,0,1:T(4,128)(2,1)} %bitcast.67), calls=%async_computation | async-start | bytes 4194304 | tf_op jit(solution)/shard_map/all_to_all | solution.py:22
  29.5 0.0 reduce-scatter.2.cloned.1.call-start
  29.6 81.0 %all-to-all-done = bf16[4,512,512]{2,0,1:T(4,128)(2,1)S(1)} async-done(((bf16[4,512,512]{2,0,1:T(4,128)(2,1)}), bf16[4,512,512]{2,0,1:T(4,128)(2,1)S(1)}, u32[]{:S(2)}, u32[]{:S(2)}) %all-to-all-start) | async-done | bytes 2097184 | tf_op jit(solution)/shard_map/all_to_all | solution.py:22
  110.6 0.4 copy.13
  111.1 1.6 copy.14
  112.6 2.3 gather_fusion
  114.9 2.3 select_convert_fusion
  117.2 0.0 reduce-scatter.2.cloned.1.call-update
  117.2 0.0 copy-start
  117.2 612.9 %reduce-scatter.2.cloned.1.call-done = f32[1,32,512]{2,1,0:T(8,128)} async-done(((f32[64,32,512]{2,1,0:T(8,128)}), f32[1,32,512]{2,1,0:T(8,128)}) %reduce-scatter.2.cloned.1.call-update) | async-done | bytes 65552 | tf_op jit(solution)/shard_map/reduce_scatter | solution.py:25
  730.1 0.8 convert_element_type.22
  730.9 68.1 %all-gather = bf16[1,512,512]{2,1,0:T(8,128)(2,1)S(1)} all-gather(bf16[1,32,512]{2,1,0:T(8,128)(2,1)S(1)} %convert_element_type.22), channel_id=2, replica_groups=mesh['rep'=64,'fsdp'=16] {'fsdp'}, dimensions={1}, use_global_device_ids=true | all-gather | bytes 557056 | tf_op jit(solution)/shard_map/all_gather | solution.py:27
  799.1 0.5 fusion.1
  799.6 1.8 fusion.12
  801.4 1.8 fusion.10
  803.3 1.8 fusion.8
  805.1 1.8 fusion.6
  807.0 0.0 copy-start.5
  807.0 0.0 copy-start.1
  807.0 1.8 fusion
  808.9 0.2 fusion.3
  809.2 0.0 copy-done.1
  809.2 0.0 copy-start.4
  809.2 0.7 fusion.21
  809.9 0.7 fusion.19
  810.6 0.7 fusion.17
  811.3 0.7 fusion.15
  812.0 0.7 fusion.2
  812.8 0.0 copy-start.3
  812.8 0.7 dynamic-slice_bitcast_fusion
  813.4 1.0 fusion.4
  (11 shorter events, 0.0 us)
Async XLA Ops:
  11.7 17.8 %copy-start.6 = (s32[64]{0:T(128)S(1)}, s32[64]{0:T(128)}, u32[]{:S(2)}) copy-start(s32[64]{0:T(128)} %param.7) | copy-start | bytes 772
  11.7 98.9 %all-to-all-start = ((bf16[4,512,512]{2,0,1:T(4,128)(2,1)}), bf16[4,512,512]{2,0,1:T(4,128)(2,1)S(1)}, u32[]{:S(2)}, u32[]{:S(2)}) async-start(bf16[4,512,512]{2,0,1:T(4,128)(2,1)} %bitcast.67), calls=%async_computation | async-start | bytes 4194304 | tf_op jit(solution)/shard_map/all_to_all | solution.py:22
  29.5 700.6 %reduce-scatter.2.cloned.1.call-start = ((), (), s32[]{:S(2)}) async-start(), calls=%async_computation.2 | async-start | bytes 4259840 | tf_op jit(solution)/shard_map/reduce_scatter | solution.py:25
  117.2 681.9 %copy-start.2 = (f32[1,512,512]{2,1,0:T(8,128)S(1)}, f32[1,512,512]{2,1,0:T(8,128)}, u32[]{:S(2)}) copy-start(f32[1,512,512]{2,1,0:T(8,128)} %param.9) | copy-start | bytes 3145732
  117.2 682.3 %copy-start = (f32[1,512,512]{2,1,0:T(8,128)S(1)}, f32[1,512,512]{2,1,0:T(8,128)}, u32[]{:S(2)}) copy-start(f32[1,512,512]{2,1,0:T(8,128)} %param.11) | copy-start | bytes 3145732
  807.0 1.9 copy-start.5
  807.0 2.1 copy-start.1
  809.2 2.9 copy-start.4
  812.8 1.7 copy-start.3
Sparse Core Ops, SparseCore 0:
  117.4 612.6 reduce-scatter.1
where the time goes:
time: 822 us; the launch traced here: 821 us
  waiting for transfers between devices  694 us (84%)
  blocking collectives  68.1 us (8%)
  starting transfers between devices  17.8 us (2%)
  matrix products  14.5 us (2%)
  between operations  14.3 us (2%)
  local copies, waits for them, and re-layouts  9.51 us (1%)
    reduce_scatter x1, waiting for transfers between devices, per_device(): summed = lax.psum_scatter(selected, 'rep', scatter_dimension=0, tiled=True)  613 us
    all_to_all x1, waiting for transfers between devices, per_device(): lax.all_to_all(local_blocks, 'fsdp', split_axis=1, concat_axis=0, tiled=T...  81 us
    all_gather x1, blocking collectives, per_device(): full_block = lax.all_gather(grad_slab, 'fsdp', axis=0, tiled=True)  68.1 us
    all_to_all x1, starting transfers between devices, per_device(): lax.all_to_all(local_blocks, 'fsdp', split_axis=1, concat_axis=0, tiled=T...  17.8 us
  transfers between devices with their start and end apart: 2, of which 2 were waited for; matrix products, arithmetic and copies ran while one was open for 0% of the time, Pallas kernels for 0%

commit v1 on v0

v1 whole, which is shorter than its diff:
```python
import jax
import jax.numpy as jnp
from jax import lax
from jax.sharding import Mesh, PartitionSpec as P

decay_rate = 0.9
REP = ("zh", "x", "y")
XY = ("x", "y")
FSDP = ("zl", "core")
f32, bf16 = jnp.float32, jnp.bfloat16


def exchange(a, axes):
    return lax.all_to_all(a, axes, split_axis=0, concat_axis=0, tiled=True)


def dot32(a, b):
    return jnp.dot(a, b, precision=lax.Precision.HIGHEST, preferred_element_type=f32)


def fifth_power(root):
    square = dot32(root, root)
    return dot32(dot32(square, square), root)


def summed_block(grad_partial, owner_block, ready):
    pieces = grad_partial[0].reshape(4, 16, 32, 512).transpose(1, 0, 2, 3)
    arrived, ready = lax.optimization_barrier((exchange(pieces, XY), ready))
    part = arrived.astype(f32).sum(0).astype(bf16)
    tiles = part.reshape(4, 4, 8, 4, 128).transpose(1, 3, 0, 2, 4).reshape(16, 4, 8, 128)
    by_block = exchange(tiles, FSDP).reshape(64, 8, 128)
    by_slot = jnp.take(by_block, owner_block, axis=0, mode="clip")
    parts = exchange(by_slot, REP).reshape(4, 16, 8, 128)
    mine = parts.astype(f32).sum(0).astype(bf16)
    own = exchange(jnp.broadcast_to(mine[None], (8, 16, 8, 128)), "zl")
    other = lax.ppermute(own, "core", [(0, 1), (1, 0)])
    first = lax.axis_index("core") == 0
    even, odd = jnp.where(first, own, other), jnp.where(first, other, own)
    tiles = jnp.stack([even, odd], axis=1).reshape(4, 4, 16, 8, 128)
    return tiles.transpose(2, 0, 3, 1, 4).reshape(512, 512), ready


def per_device(grad_partial, owner_block, left_stat, right_stat, left_root, right_root):
    gram_weight = (1.0 - decay_rate) / 512
    fifths = (fifth_power(left_root[0]), fifth_power(right_root[0]))
    block, (left_fifth, right_fifth) = summed_block(grad_partial, owner_block, fifths)
    start = (lax.axis_index("zl") * 2 + lax.axis_index("core")) * 32

    def rows(a):
        return lax.dynamic_slice_in_dim(a, start, 32, 0)

    left_new = decay_rate * left_stat[0] + gram_weight * lax.dot_general(
        rows(block), block, (((1,), (1,)), ((), ())), preferred_element_type=f32
    )
    left_next = (5.0 * rows(left_root[0]) - dot32(left_new, left_fifth)) / 4.0
    right_full = decay_rate * right_stat[0] + gram_weight * lax.dot_general(
        block, block, (((0,), (0,)), ((), ())), preferred_element_type=f32
    )
    right_next_full = (5.0 * right_root[0] - dot32(right_full, right_fifth)) / 4.0
    left_half = jnp.dot(left_next.astype(bf16), block, preferred_element_type=f32).astype(bf16)
    result = jnp.dot(left_half, right_next_full.astype(bf16), preferred_element_type=f32).astype(bf16)
    return (result[None], left_new[None], rows(right_full)[None], left_next[None], rows(right_next_full)[None])


def solution(mesh):
    fine = Mesh(mesh.devices.reshape(4, 4, 4, 8, 2), REP + FSDP)
    in_specs = (
        P(REP, FSDP, None, None),
        P(),
        P(REP, FSDP, None),
        P(REP, None, None),
        P(REP, None, None),
        P(REP, None, None),
    )
    return jax.shard_map(
        per_device, mesh=fine, in_specs=in_specs, out_specs=(P(REP, FSDP, None),) * 5, check_vma=False
    )
```

time: 822 us -> 160 us (0.19)
  waiting for transfers between devices: 694 us -> 18 us
  starting transfers between devices: 17.8 us -> 41.3 us
  between operations: 14.3 us -> 0.86 us
    reduce_scatter x1 -> x0, waiting for transfers between devices: 613 us -> none  [per_device(): summed = lax.psum_scatter(selected, 'rep', scatter_dimension=0, tiled=True)]
    all_to_all x0 -> x2, blocking collectives: none -> 71.7 us  [exchange(): return lax.all_to_all(a, axes, split_axis=0, concat_axis=0, tiled=True)]
    all_gather x1 -> x0, blocking collectives: 68.1 us -> none  [per_device(): full_block = lax.all_gather(grad_slab, 'fsdp', axis=0, tiled=True)]
    all_to_all x1 -> x2, waiting for transfers between devices: 81 us -> 16.9 us  [exchange(): return lax.all_to_all(a, axes, split_axis=0, concat_axis=0, tiled=True)]
    all_to_all x1 -> x2, starting transfers between devices: 17.8 us -> 33.7 us  [exchange(): return lax.all_to_all(a, axes, split_axis=0, concat_axis=0, tiled=True)]
    dot_general x13 -> x11, matrix products: 14.5 us -> 19.8 us  [the longest x8 15.6 us: dot32(): jnp.dot(a, b, precision=lax.Precision.HIGHEST, preferred_element_type=f32)]
  transfers between devices with their start and end apart: 2 -> 3, of which waited for: 2 -> 3; matrix products, arithmetic and copies ran while one was open for 0% -> 8% of each run, Pallas kernels for 0% -> 0%
where the time goes in v1:
time: 160 us; the launch traced here: 159 us
  blocking collectives  71.7 us (45%)
  starting transfers between devices  41.3 us (26%)
  matrix products  19.8 us (12%)
  waiting for transfers between devices  18 us (11%)
  local copies, waits for them, and re-layouts  5.4 us (3%)
  other arithmetic  2.1 us (1%)
    all_to_all x2, blocking collectives, exchange(): return lax.all_to_all(a, axes, split_axis=0, concat_axis=0, tiled=True)  71.7 us
    all_to_all x2, starting transfers between devices, exchange(): return lax.all_to_all(a, axes, split_axis=0, concat_axis=0, tiled=True)  33.7 us
    all_to_all x2, waiting for transfers between devices, exchange(): return lax.all_to_all(a, axes, split_axis=0, concat_axis=0, tiled=True)  16.9 us
    dot_general x8, matrix products, dot32(): jnp.dot(a, b, precision=lax.Precision.HIGHEST, preferred_element_type=f32)  15.6 us
    ppermute x1, starting transfers between devices, summed_block(): other = lax.ppermute(own, 'core', [(0, 1), (1, 0)])  7.61 us
  transfers between devices with their start and end apart: 3, of which 3 were waited for; matrix products, arithmetic and copies ran while one was open for 8% of the time, Pallas kernels for 0%

profile of v1, /device:TPU:1, one launch (start us, length us, event | category | flops | bytes accessed | tf_op | source)
XLA Modules:
  0.0 159.3 jit_solution(15851702869131517919)
XLA Ops:
  0.6 3.2 %copy.19 = bf16[16,4,32,512]{3,2,1,0:T(8,128)(2,1)} copy(bf16[16,4,32,512]{3,2,0,1:T(8,128)(2,1)} %bitcast.64) | data formatting | bytes 4194304 | tf_op jit(solution)/shard_map/transpose | solution.py:27
  3.8 7.8 %all-to-all-start = ((bf16[16,4,32,512]{3,2,1,0:T(8,128)(2,1)}), bf16[16,4,32,512]{3,2,1,0:T(8,128)(2,1)}, u32[]{:S(2)}, u32[]{:S(2)}) async-start(bf16[16,4,32,512]{3,2,1,0:T(8,128)(2,1)} %copy.19), calls=%async_computation | async-start | bytes 4194304 | tf_op jit(solution)/shard_map/all_to_all | solution.py:14
  11.6 0.0 copy-done.1
  11.6 1.8 %fusion.11 = f32[512,512]{1,0:T(8,128)S(1)} fusion(f32[1,512,512]{2,1,0:T(8,128)S(1)} %copy-done.1), kind=kOutput, calls=%fused_computation.19 | convolution fusion | flops 1610612736 | bytes 2097152 | tf_op jit(solution)/shard_map/dot_general | solution.py:18
  13.4 1.8 %fusion.7 = f32[512,512]{1,0:T(8,128)S(1)} fusion(f32[1,512,512]{2,1,0:T(8,128)S(1)} %copy-done), kind=kOutput, calls=%fused_computation.15 | convolution fusion | flops 1610612736 | bytes 2097152 | tf_op jit(solution)/shard_map/dot_general | solution.py:18
  15.3 1.8 %fusion.18 = f32[512,512]{1,0:T(8,128)S(1)} fusion(f32[512,512]{1,0:T(8,128)S(1)} %fusion.11), kind=kOutput, calls=%fused_computation.31 | convolution fusion | flops 1610612736 | bytes 2097152 | tf_op jit(solution)/shard_map/dot_general | solution.py:18
  17.1 2.8 %fusion.9 = f32[512,512]{1,0:T(8,128)} fusion(f32[512,512]{1,0:T(8,128)S(1)} %fusion.18, f32[1,512,512]{2,1,0:T(8,128)S(1)} %copy-done.1), kind=kOutput, calls=%fused_computation.17 | convolution fusion | flops 1610612736 | bytes 3145728 | tf_op jit(solution)/shard_map/dot_general | solution.py:18
  19.9 1.8 %fusion.19 = f32[512,512]{1,0:T(8,128)S(1)} fusion(f32[512,512]{1,0:T(8,128)S(1)} %fusion.7), kind=kOutput, calls=%fused_computation.32 | convolution fusion | flops 1610612736 | bytes 2097152 | tf_op jit(solution)/shard_map/dot_general | solution.py:18
  21.8 2.9 %fusion.5 = f32[512,512]{1,0:T(8,128)} fusion(f32[512,512]{1,0:T(8,128)S(1)} %fusion.19, f32[1,512,512]{2,1,0:T(8,128)S(1)} %copy-done), kind=kOutput, calls=%fused_computation.13 | convolution fusion | flops 1610612736 | bytes 3145728 | tf_op jit(solution)/shard_map/dot_general | solution.py:18
  24.7 4.9 %all-to-all-done = bf16[16,4,32,512]{3,2,1,0:T(8,128)(2,1)} async-done(((bf16[16,4,32,512]{3,2,1,0:T(8,128)(2,1)}), bf16[16,4,32,512]{3,2,1,0:T(8,128)(2,1)}, u32[]{:S(2)}, u32[]{:S(2)}) %all-to-all-start) | async-done | bytes 2097184 | tf_op jit(solution)/shard_map/all_to_all | solution.py:14
  29.5 2.0 %reduce_sum.24 = bf16[4,32,512]{2,1,0:T(8,128)(2,1)S(1)} reduce(bf16[16,4,32,512]{3,2,1,0:T(8,128)(2,1)} %all-to-all-done, bf16[]{:T(256)} %constant.32.clone.1), dimensions={0}, to_apply=%region_0.0 | reduce | flops 983040 | bytes 2228226 | tf_op jit(solution)/shard_map/reduce_sum | solution.py:29
  31.5 0.7 copy.20
  32.2 26.0 %all-to-all-start.1 = ((bf16[16,4,8,128]{3,2,1,0:T(8,128)(2,1)}), bf16[16,4,8,128]{3,2,1,0:T(8,128)(2,1)S(1)}, u32[]{:S(2)}, u32[]{:S(2)}) async-start(bf16[16,4,8,128]{3,2,1,0:T(8,128)(2,1)} %copy.20), calls=%async_computation.1 | async-start | bytes 262144 | tf_op jit(solution)/shard_map/all_to_all | solution.py:14
  58.2 12.0 %all-to-all-done.1 = bf16[16,4,8,128]{3,2,1,0:T(8,128)(2,1)S(1)} async-done(((bf16[16,4,8,128]{3,2,1,0:T(8,128)(2,1)}), bf16[16,4,8,128]{3,2,1,0:T(8,128)(2,1)S(1)}, u32[]{:S(2)}, u32[]{:S(2)}) %all-to-all-start.1) | async-done | bytes 131104 | tf_op jit(solution)/shard_map/all_to_all | solution.py:14
  70.2 0.6 gather_fusion
  70.8 49.4 %all_to_all.20 = bf16[64,8,128]{2,1,0:T(8,128)(2,1)S(1)} all-to-all(bf16[64,8,128]{2,1,0:T(8,128)(2,1)S(1)} %gather_fusion), channel_id=1, replica_groups=mesh['zh'=4,'x'=4,'y'=4,'zl'=8,'core'=2] {'zh','x','y'}, dimensions={0} | all-to-all | bytes 262144 | tf_op jit(solution)/shard_map/all_to_all | solution.py:14
  120.3 22.3 %all_to_all.21 = bf16[8,16,8,128]{3,2,1,0:T(8,128)(2,1)S(1)} all-to-all(bf16[8,16,8,128]{3,2,1,0:T(8,128)(2,1)S(1)} %broadcast_in_dim.26), channel_id=1, replica_groups=mesh['zh'=4,'x'=4,'y'=4,'zl'=8,'core'=2] {'zl'}, dimensions={0} | all-to-all | bytes 524288 | tf_op jit(solution)/shard_map/all_to_all | solution.py:14
  142.6 7.6 %collective-permute-start = (bf16[8,16,8,128]{3,2,1,0:T(8,128)(2,1)S(1)}, bf16[8,16,8,128]{3,2,1,0:T(8,128)(2,1)S(1)}, u32[]{:S(2)}, u32[]{:S(2)}) collective-permute-start(bf16[8,16,8,128]{3,2,1,0:T(8,128)(2,1)S(1)} %all_to_all.21), channel_id=1, source_target_pairs={{0,1},{1,0},{2,3},{3,2},{4,5},{5,4},{6,7},{7,6},{8,9},{9,8},{10,11... | collective-permute-start | bytes 786440 | tf_op jit(solution)/shard_map/ppermute | solution.py:36
  150.2 1.1 collective-permute-done
  151.4 0.1 pad_maximum_fusion
  151.5 0.1 copy.22
  151.6 1.8 %fusion.1 = f32[512,512]{1,0:T(8,128)S(1)} fusion(bf16[512,512]{1,0:T(8,128)(2,1)S(1)} %bitcast.61, f32[1,512,512]{2,1,0:T(8,128)} %param.9), kind=kOutput, calls=%fused_computation.4 | convolution fusion | flops 269221888 | bytes 2621440 | tf_op jit(solution)/shard_map/dot_general | solution.py:56
  153.4 0.0 copy-start.7
  153.4 1.9 %fusion = f32[512,512]{1,0:T(8,128)S(1)} fusion(f32[512,512]{1,0:T(8,128)S(1)} %fusion.1, f32[512,512]{1,0:T(8,128)S(1)} %copy-done.4, f32[1,512,512]{2,1,0:T(8,128)S(1)} %copy-done), kind=kOutput, calls=%fused_computation.2 | convolution fusion | flops 1611399168 | bytes 4194304 | tf_op jit(solution)/shard_map/dot_general | solution.py:18
  155.3 0.2 fusion.3
  155.6 0.0 copy-start.5
  155.6 0.7 dynamic-slice_bitcast_fusion
  156.3 0.0 copy-done.3
  156.3 0.7 fusion.2
  157.0 0.0 copy-start.6
  157.1 2.2 %fusion.4 = bf16[1,32,512]{2,1,0:T(8,128)(2,1)} fusion(bf16[512,512]{1,0:T(8,128)(2,1)S(1)} %bitcast.63, f32[512,512]{1,0:T(8,128)} %copy-done.2, f32[32,512]{1,0:T(8,128)S(1)} %fusion.2), kind=kOutput, calls=%fused_computation.11 | convolution fusion | flops 33865728 | bytes 1671168 | tf_op jit(solution)/shard_map/dot_general | solution.py:61
  159.3 0.0 copy-done.6
  (16 shorter events, 0.1 us)
Async XLA Ops:
  3.8 7.8 %copy-start.1 = (f32[1,512,512]{2,1,0:T(8,128)S(1)}, f32[1,512,512]{2,1,0:T(8,128)}, u32[]{:S(2)}) copy-start(f32[1,512,512]{2,1,0:T(8,128)} %param.10) | copy-start | bytes 3145732
  3.8 9.6 %copy-start = (f32[1,512,512]{2,1,0:T(8,128)S(1)}, f32[1,512,512]{2,1,0:T(8,128)}, u32[]{:S(2)}) copy-start(f32[1,512,512]{2,1,0:T(8,128)} %param.11) | copy-start | bytes 3145732
  3.8 25.7 %all-to-all-start = ((bf16[16,4,32,512]{3,2,1,0:T(8,128)(2,1)}), bf16[16,4,32,512]{3,2,1,0:T(8,128)(2,1)}, u32[]{:S(2)}, u32[]{:S(2)}) async-start(bf16[16,4,32,512]{3,2,1,0:T(8,128)(2,1)} %copy.19), calls=%async_computation | async-start | bytes 4194304 | tf_op jit(solution)/shard_map/all_to_all | solution.py:14
  24.6 33.5 %copy-start.8 = (s32[64]{0:T(128)S(1)}, s32[64]{0:T(128)}, u32[]{:S(2)}) copy-start(s32[64]{0:T(128)} %param.7) | copy-start | bytes 772
  32.2 38.0 %all-to-all-start.1 = ((bf16[16,4,8,128]{3,2,1,0:T(8,128)(2,1)}), bf16[16,4,8,128]{3,2,1,0:T(8,128)(2,1)S(1)}, u32[]{:S(2)}, u32[]{:S(2)}) async-start(bf16[16,4,8,128]{3,2,1,0:T(8,128)(2,1)} %copy.20), calls=%async_computation.1 | async-start | bytes 262144 | tf_op jit(solution)/shard_map/all_to_all | solution.py:14
  142.6 8.8 %collective-permute-start = (bf16[8,16,8,128]{3,2,1,0:T(8,128)(2,1)S(1)}, bf16[8,16,8,128]{3,2,1,0:T(8,128)(2,1)S(1)}, u32[]{:S(2)}, u32[]{:S(2)}) collective-permute-start(bf16[8,16,8,128]{3,2,1,0:T(8,128)(2,1)S(1)} %all_to_all.21), channel_id=1, source_target_pairs={{0,1},{1,0},{2,3},{3,2},{4,5},{5,4},{6,7},{7,6},{8,9},{9,8},{10,11... | collective-permute-start | bytes 786440 | tf_op jit(solution)/shard_map/ppermute | solution.py:36
  151.5 1.9 %copy-start.4 = (f32[512,512]{1,0:T(8,128)S(1)}, f32[512,512]{1,0:T(8,128)}, u32[]{:S(2)}) copy-start(f32[512,512]{1,0:T(8,128)} %fusion.5) | copy-start | bytes 3145732
  153.4 1.9 %copy-start.7 = (f32[1,32,512]{2,1,0:T(8,128)S(1)}, f32[1,32,512]{2,1,0:T(8,128)}, u32[]{:S(2)}) copy-start(f32[1,32,512]{2,1,0:T(8,128)} %param.8) | copy-start | bytes 196612
  153.4 2.9 %copy-start.3 = (f32[512,512]{1,0:T(8,128)S(1)}, f32[512,512]{1,0:T(8,128)}, u32[]{:S(2)}) copy-start(f32[512,512]{1,0:T(8,128)} %fusion.9) | copy-start | bytes 3145732
  155.3 1.0 copy-start.2
  155.6 3.7 %copy-start.5 = (f32[32,512]{1,0:T(8,128)}, f32[32,512]{1,0:T(8,128)S(1)}, u32[]{:S(2)}) copy-start(f32[32,512]{1,0:T(8,128)S(1)} %fusion.3) | copy-start | bytes 196612
  157.0 2.2 %copy-start.6 = (f32[32,512]{1,0:T(8,128)}, f32[32,512]{1,0:T(8,128)S(1)}, u32[]{:S(2)}) copy-start(f32[32,512]{1,0:T(8,128)S(1)} %fusion.2) | copy-start | bytes 196612

commit v2 on v1

v2 whole, which is shorter than its diff:
```python
import jax
import jax.numpy as jnp
from jax import lax
from jax.experimental import pallas as pl
from jax.experimental.pallas import tpu as pltpu
from jax.sharding import Mesh, PartitionSpec as P

decay_rate = 0.9
REP = ("zh", "x", "y")
XY = ("x", "y")
FSDP = ("zl", "core")
f32, bf16 = jnp.float32, jnp.bfloat16
VMEM = pl.BlockSpec(memory_space=pltpu.VMEM)
SMEM = pl.BlockSpec(memory_space=pltpu.SMEM)
HBM = pl.BlockSpec(memory_space=pltpu.HBM)


def exchange(a, axes):
    return lax.all_to_all(a, axes, split_axis=0, concat_axis=0, tiled=True)


def dot(a, b, contract=((1,), (0,))):
    return lax.dot_general(a, b, (contract, ((), ())), preferred_element_type=f32)


def halves(a):
    high = a.astype(bf16)
    return high, (a - high.astype(f32)).astype(bf16)


def dot3(a, b):
    return dot(a[0], b[0]) + (dot(a[0], b[1]) + dot(a[1], b[0]))


def regroup_kernel(blocks, pieces):
    for q in range(4):
        pieces[:, q] = blocks[q]


def regroup(blocks):
    return pl.pallas_call(
        regroup_kernel,
        out_shape=jax.ShapeDtypeStruct((16, 4, 32, 512), bf16),
        in_specs=[VMEM],
        out_specs=VMEM,
        compiler_params=pltpu.CompilerParams(vmem_limit_bytes=6 * 2**20),
        name="regroup",
    )(blocks)


def sum_kernel(arrived, tiles):
    for q in range(4):
        total = arrived[0, q].astype(f32)
        for source in range(1, 16):
            total = total + arrived[source, q].astype(f32)
        for piece in range(16):
            row, column = piece // 4 * 8, piece % 4 * 128
            tiles[piece, q] = total[row : row + 8, column : column + 128].astype(bf16)


def sum_to_tiles(arrived):
    return pl.pallas_call(
        sum_kernel,
        out_shape=jax.ShapeDtypeStruct((16, 4, 8, 128), bf16),
        in_specs=[VMEM],
        out_specs=VMEM,
        compiler_params=pltpu.CompilerParams(vmem_limit_bytes=8 * 2**20),
        name="sum_to_tiles",
    )(arrived)


def powers_kernel(left_root, right_root, powers):
    for side, root in enumerate((left_root, right_root)):
        first = halves(root[...])
        square = halves(dot3(first, first))
        fourth = halves(dot3(square, square))
        powers[2 * side], powers[2 * side + 1] = halves(dot3(fourth, first))


def fifth_powers(left_root, right_root):
    return pl.pallas_call(
        powers_kernel,
        out_shape=jax.ShapeDtypeStruct((4, 512, 512), bf16),
        in_specs=[VMEM] * 2,
        out_specs=VMEM,
        compiler_params=pltpu.CompilerParams(vmem_limit_bytes=10 * 2**20),
        cost_estimate=pl.CostEstimate(flops=18 * 2 * 512**3, bytes_accessed=4 * 2**20, transcendentals=0),
        name="fifth_powers",
    )(left_root, right_root)


def tail_kernel(
    place, own, left_stat, left_rows, right_stat, right_root, other_hbm, powers_hbm,
    result, left_new, right_new, left_next, right_next, other, powers, grid, full, sems,
):
    pairs = ((other_hbm, other), (powers_hbm, powers))
    copies = [pltpu.make_async_copy(*pair, sems.at[i]) for i, pair in enumerate(pairs)]
    for copy in copies:
        copy.start()
    core, mine = place[0], place[1]
    gram_weight = (1.0 - decay_rate) / 512
    for tiles, parity in ((own, core), (other, 1 - core)):
        if tiles is other:
            copies[0].wait()
        for chip in range(8):
            column = pl.multiple_of((chip % 2 * 2 + parity) * 128, 128)
            grid[:, pl.ds(chip // 2 * 8, 8), pl.ds(column, 128)] = tiles[chip].astype(f32)
    block = grid[...].reshape(512, 512).astype(bf16)
    stat = decay_rate * right_stat[...] + gram_weight * dot(block, block, ((0,), (0,)))
    full[...] = stat
    rows = grid[mine].astype(bf16)
    stat_rows = decay_rate * left_stat[...] + gram_weight * dot(rows, block, ((1,), (1,)))
    left_new[...] = stat_rows
    copies[1].wait()
    product = dot3(halves(stat_rows), (powers[0], powers[1]))
    next_rows = (5.0 * left_rows[...] - product) / 4.0
    left_next[...] = next_rows
    left_half = dot(next_rows.astype(bf16), block).astype(bf16)
    start = pl.multiple_of(mine * 32, 32)
    right_new[...] = full[pl.ds(start, 32)]
    root = (5.0 * right_root[...] - dot3(halves(stat), (powers[2], powers[3]))) / 4.0
    full[...] = root
    right_next[...] = full[pl.ds(start, 32)]
    result[...] = dot(left_half, root.astype(bf16)).astype(bf16)


def tail(place, *operands):
    rows, whole = (32, 512), (512, 512)
    return pl.pallas_call(
        tail_kernel,
        out_shape=(jax.ShapeDtypeStruct(rows, bf16),) + (jax.ShapeDtypeStruct(rows, f32),) * 4,
        in_specs=[SMEM] + [VMEM] * 5 + [HBM] * 2,
        out_specs=(VMEM,) * 5,
        scratch_shapes=[
            pltpu.VMEM((8, 16, 8, 128), bf16), pltpu.VMEM((4, 512, 512), bf16),
            pltpu.VMEM((16, 32, 512), f32), pltpu.VMEM(whole, f32), pltpu.SemaphoreType.DMA((2,)),
        ],
        compiler_params=pltpu.CompilerParams(vmem_limit_bytes=14 * 2**20),
        name="tail",
    )(place, *operands)


def held(*arrays):
    return lax.optimization_barrier(arrays)


def gathered_tiles(grad_partial, owner_block, left_root, right_root):
    pieces = regroup(grad_partial.reshape(4, 16, 32, 512))
    arrived = exchange(pieces.reshape(16, 128, 512), XY)
    arrived, owner_block, left_root, right_root = held(arrived, owner_block, left_root, right_root)
    by_block = exchange(sum_to_tiles(arrived.reshape(16, 4, 32, 512)), FSDP).reshape(64, 8, 128)
    by_block, owner_block = held(by_block, owner_block)
    by_slot = jnp.take(by_block, owner_block, axis=0, mode="clip")
    by_slot, left_root, right_root = held(by_slot, left_root, right_root)
    powers = fifth_powers(left_root, right_root)
    parts, powers = held(exchange(by_slot, REP), powers)
    mine = parts.reshape(4, 16, 8, 128).astype(f32).sum(0).astype(bf16)
    own = exchange(jnp.broadcast_to(mine[None], (8, 16, 8, 128)), "zl")
    return own, lax.ppermute(own, "core", [(0, 1), (1, 0)]), powers


def per_device(grad_partial, owner_block, left_stat, right_stat, left_root, right_root):
    own, other, powers = gathered_tiles(grad_partial, owner_block, left_root[0], right_root[0])
    core = lax.axis_index("core")
    mine = lax.axis_index("zl") * 2 + core
    left_rows = lax.dynamic_slice_in_dim(left_root[0], mine * 32, 32, 0)
    outs = tail(
        jnp.stack([core, mine]).astype(jnp.int32), own, left_stat[0], left_rows,
        right_stat[0], right_root[0], other, powers,
    )
    return tuple(out[None] for out in outs)


def solution(mesh):
    fine = Mesh(mesh.devices.reshape(4, 4, 4, 8, 2), REP + FSDP)
    in_specs = (
        P(REP, FSDP, None, None),
        P(),
        P(REP, FSDP, None),
        P(REP, None, None),
        P(REP, None, None),
        P(REP, None, None),
    )
    return jax.shard_map(
        per_device, mesh=fine, in_specs=in_specs, out_specs=(P(REP, FSDP, None),) * 5, check_vma=False
    )
```

time: 160 us -> 152 us (0.950)
  matrix products: 19.8 us -> 0 us
  blocking collectives: 71.7 us -> 83.1 us
  starting transfers between devices: 41.3 us -> 31.1 us
  Pallas kernels: 0 us -> 9.93 us
  local copies, waits for them, and re-layouts: 5.4 us -> 7.42 us
  other arithmetic: 2.1 us -> 0.1 us
    dot_general x11 -> x0, matrix products: 19.8 us -> none  [the longest x8 15.6 us: dot32(): jnp.dot(a, b, precision=lax.Precision.HIGHEST, preferred_element_type=f32)]
    all_to_all x2 -> x3, blocking collectives: 71.7 us -> 83.1 us  [exchange(): return lax.all_to_all(a, axes, split_axis=0, concat_axis=0, tiled=True)]
    all_to_all x2 -> x1, starting transfers between devices: 33.7 us -> 23.5 us  [exchange(): return lax.all_to_all(a, axes, split_axis=0, concat_axis=0, tiled=True)]
    pallas_call x0 -> x4, Pallas kernels: none -> 9.93 us  [the longest x1 5.21 us: fifth_powers(): pl.pallas_call(powers_kernel, out_shape=jax.ShapeDtypeStruct((4, 512, 512...]
    unnamed x18 -> x14, local copies, waits for them, and re-layouts: 0.05 us -> 5.26 us
    transpose x2 -> x0, local copies, waits for them, and re-layouts: 3.29 us -> none  [the longest x1 3.16 us: summed_block(): pieces = grad_partial[0].reshape(4, 16, 32, 512).transpose(1, 0, 2, 3)]
    reduce_sum x2 -> x1, other arithmetic: 2 us -> 0.02 us  [gathered_tiles(): mine = parts.reshape(4, 16, 8, 128).astype(f32).sum(0).astype(bf16)]
    all_to_all x2 -> x1, waiting for transfers between devices: 16.9 us -> 18.7 us  [exchange(): return lax.all_to_all(a, axes, split_axis=0, concat_axis=0, tiled=True)]
  transfers between devices with their start and end apart: 3 -> 2, of which waited for: 3 -> 2; matrix products, arithmetic and copies ran while one was open for 8% -> 1% of each run, Pallas kernels for 0% -> 3%
where the time goes in v2:
time: 152 us; the launch traced here: 151 us
  blocking collectives  83.1 us (55%)
  starting transfers between devices  31.1 us (20%)
  waiting for transfers between devices  19.1 us (13%)
  Pallas kernels  9.93 us (7%)
  local copies, waits for them, and re-layouts  7.42 us (5%)
    all_to_all x3, blocking collectives, exchange(): return lax.all_to_all(a, axes, split_axis=0, concat_axis=0, tiled=True)  83.1 us
    all_to_all x1, starting transfers between devices, exchange(): return lax.all_to_all(a, axes, split_axis=0, concat_axis=0, tiled=True)  23.5 us
    all_to_all x1, waiting for transfers between devices, exchange(): return lax.all_to_all(a, axes, split_axis=0, concat_axis=0, tiled=True)  18.7 us
    ppermute x1, starting transfers between devices, gathered_tiles(): return (own, lax.ppermute(own, 'core', [(0, 1), (1, 0)]), powers)  7.61 us
    unnamed x14, local copies, waits for them, and re-layouts  5.26 us
    pallas_call x1, Pallas kernels, fifth_powers(): pl.pallas_call(powers_kernel, out_shape=jax.ShapeDtypeStruct((4, 512, 512...  5.21 us
    pallas_call x1, Pallas kernels, tail(): pl.pallas_call(tail_kernel, out_shape=(jax.ShapeDtypeStruct(rows, bf16),)...  4.31 us
  transfers between devices with their start and end apart: 2, of which 2 were waited for; matrix products, arithmetic and copies ran while one was open for 1% of the time, Pallas kernels for 3%

profile of v2, /device:TPU:1, one launch (start us, length us, event | category | flops | bytes accessed | tf_op | source)
XLA Modules:
  0.0 151.4 jit_solution(8044207669804263890)
XLA Ops:
  0.6 0.0 copy-start
  0.6 1.6 %copy-done = bf16[1,4,512,512]{3,2,1,0:T(8,128)(2,1)S(1)} copy-done((bf16[1,4,512,512]{3,2,1,0:T(8,128)(2,1)S(1)}, bf16[1,4,512,512]{3,2,1,0:T(8,128)(2,1)}, u32[]{:S(2)}) %copy-start) | copy-done | bytes 2097176
  2.2 0.1 regroup.1
  2.4 26.2 %all_to_all.20 = bf16[16,128,512]{2,1,0:T(8,128)(2,1)S(1)} all-to-all(bf16[16,128,512]{2,1,0:T(8,128)(2,1)S(1)} %bitcast.19), channel_id=1, replica_groups=mesh['zh'=4,'x'=4,'y'=4,'zl'=8,'core'=2] {'x','y'}, dimensions={0} | all-to-all | bytes 4194304 | tf_op jit(solution)/shard_map/all_to_all | solution.py:19
  28.5 0.0 copy-start.6
  28.5 0.3 sum_to_tiles.1
  28.8 34.8 %all_to_all.21 = bf16[16,4,8,128]{3,2,1,0:T(8,128)(2,1)S(1)} all-to-all(bf16[16,4,8,128]{3,2,1,0:T(8,128)(2,1)S(1)} %sum_to_tiles.1), channel_id=1, replica_groups=mesh['zh'=4,'x'=4,'y'=4,'zl'=8,'core'=2] {'zl','core'}, dimensions={0} | all-to-all | bytes 262144 | tf_op jit(solution)/shard_map/all_to_all | solution.py:19
  63.6 0.0 copy-done.6
  63.6 1.3 gather_fusion
  64.9 23.5 %all-to-all-start.2 = ((bf16[64,8,128]{2,1,0:T(8,128)(2,1)}), bf16[64,8,128]{2,1,0:T(8,128)(2,1)S(1)}, u32[]{:S(2)}, u32[]{:S(2)}) async-start(bf16[64,8,128]{2,1,0:T(8,128)(2,1)} %gather_fusion), calls=%async_computation.2 | async-start | bytes 262144 | tf_op jit(solution)/shard_map/all_to_all | solution.py:19
  88.4 0.0 copy-start.2
  88.4 1.2 copy-done.2
  89.6 0.0 copy-start.5
  89.6 1.2 copy-done.5
  90.8 0.0 copy-start.1
  90.8 0.0 copy-start.4
  90.8 5.2 %fifth_powers.1.powers_hbm = bf16[4,512,512]{2,1,0:T(8,128)(2,1)S(1)} custom-call(f32[512,512]{1,0:T(8,128)S(1)} %bitcast.25, f32[512,512]{1,0:T(8,128)S(1)} %bitcast.22), custom_call_target="tpu_custom_call" | custom-call | flops 4831838208 | bytes 4194304 | tf_op jit(solution)/shard_map/fifth_powers/pallas_call | solution.py:81
  96.0 18.7 %all-to-all-done.2 = bf16[64,8,128]{2,1,0:T(8,128)(2,1)S(1)} async-done(((bf16[64,8,128]{2,1,0:T(8,128)(2,1)}), bf16[64,8,128]{2,1,0:T(8,128)(2,1)S(1)}, u32[]{:S(2)}, u32[]{:S(2)}) %all-to-all-start.2) | async-done | bytes 131104 | tf_op jit(solution)/shard_map/all_to_all | solution.py:19
  114.8 22.2 %all_to_all.22.own = bf16[8,16,8,128]{3,2,1,0:T(8,128)(2,1)S(1)} all-to-all(bf16[8,16,8,128]{3,2,1,0:T(8,128)(2,1)S(1)} %broadcast_in_dim.26), channel_id=1, replica_groups=mesh['zh'=4,'x'=4,'y'=4,'zl'=8,'core'=2] {'zl'}, dimensions={0} | all-to-all | bytes 524288 | tf_op jit(solution)/shard_map/all_to_all | solution.py:19
  137.0 7.6 %collective-permute-start = (bf16[8,16,8,128]{3,2,1,0:T(8,128)(2,1)S(1)}, bf16[8,16,8,128]{3,2,1,0:T(8,128)(2,1)}, u32[]{:S(2)}, u32[]{:S(2)}) collective-permute-start(bf16[8,16,8,128]{3,2,1,0:T(8,128)(2,1)S(1)} %all_to_all.22.own), channel_id=1, source_target_pairs={{0,1},{1,0},{2,3},{3,2},{4,5},{5,4},{6,7},{7,6},{8,9},{9,8},{10,11... | collective-permute-start | bytes 786440 | tf_op jit(solution)/shard_map/ppermute | solution.py:159
  144.6 0.1 pad_add_fusion.place
  144.7 0.8 dynamic-slice_bitcast_fusion.left_rows
  145.6 0.3 collective-permute-done.other_hbm
  145.9 0.0 copy-done.1
  145.9 0.0 copy-done.4
  145.9 0.0 copy-start.3
  145.9 1.2 copy-done.3
  147.1 4.3 %tail.1 = (bf16[32,512]{1,0:T(8,128)(2,1)}, f32[32,512]{1,0:T(8,128)}, f32[32,512]{1,0:T(8,128)}, f32[32,512]{1,0:T(8,128)}, f32[32,512]{1,0:T(8,128)}) custom-call(s32[2]{0:T(128)S(1)} %pad_add_fusion.place, bf16[8,16,8,128]{3,2,1,0:T(8,128)(2,1)S(1)} %all_to_all.22.own, f32[32,512]{1,0:T(8,128)S(1)} %bitcast.24, ...), custom_call_target="tpu_custom_call" | custom-call | tf_op jit(solution)/shard_map/tail/pallas_call | solution.py:129
  (3 shorter events, 0.1 us)
Async XLA Ops:
  0.6 1.6 %copy-start = (bf16[1,4,512,512]{3,2,1,0:T(8,128)(2,1)S(1)}, bf16[1,4,512,512]{3,2,1,0:T(8,128)(2,1)}, u32[]{:S(2)}) copy-start(bf16[1,4,512,512]{3,2,1,0:T(8,128)(2,1)} %param.6) | copy-start | bytes 6291460
  28.5 35.1 %copy-start.6 = (s32[64]{0:T(128)S(1)}, s32[64]{0:T(128)}, u32[]{:S(2)}) copy-start(s32[64]{0:T(128)} %param.7) | copy-start | bytes 772
  64.9 49.9 %all-to-all-start.2 = ((bf16[64,8,128]{2,1,0:T(8,128)(2,1)}), bf16[64,8,128]{2,1,0:T(8,128)(2,1)S(1)}, u32[]{:S(2)}, u32[]{:S(2)}) async-start(bf16[64,8,128]{2,1,0:T(8,128)(2,1)} %gather_fusion), calls=%async_computation.2 | async-start | bytes 262144 | tf_op jit(solution)/shard_map/all_to_all | solution.py:19
  88.4 1.2 copy-start.2
  89.6 1.2 copy-start.5
  90.8 55.1 %copy-start.1 = (f32[1,512,512]{2,1,0:T(8,128)S(1)}, f32[1,512,512]{2,1,0:T(8,128)}, u32[]{:S(2)}) copy-start(f32[1,512,512]{2,1,0:T(8,128)} %param.9) | copy-start | bytes 3145732
  90.8 55.1 %copy-start.4 = (f32[1,32,512]{2,1,0:T(8,128)S(1)}, f32[1,32,512]{2,1,0:T(8,128)}, u32[]{:S(2)}) copy-start(f32[1,32,512]{2,1,0:T(8,128)} %param.8) | copy-start | bytes 196612
  137.0 8.9 %collective-permute-start = (bf16[8,16,8,128]{3,2,1,0:T(8,128)(2,1)S(1)}, bf16[8,16,8,128]{3,2,1,0:T(8,128)(2,1)}, u32[]{:S(2)}, u32[]{:S(2)}) collective-permute-start(bf16[8,16,8,128]{3,2,1,0:T(8,128)(2,1)S(1)} %all_to_all.22.own), channel_id=1, source_target_pairs={{0,1},{1,0},{2,3},{3,2},{4,5},{5,4},{6,7},{7,6},{8,9},{9,8},{10,11... | collective-permute-start | bytes 786440 | tf_op jit(solution)/shard_map/ppermute | solution.py:159
  145.9 1.2 copy-start.3

commit v3 on v2

v3 whole, which is shorter than its diff:
```python
import jax
import jax.numpy as jnp
from jax import lax
from jax.experimental import pallas as pl
from jax.experimental.pallas import tpu as pltpu
from jax.sharding import Mesh, PartitionSpec as P

decay_rate = 0.9
REP = ("zh", "x", "y")
FSDP = ("zl", "core")
f32, bf16 = jnp.float32, jnp.bfloat16
VMEM = pl.BlockSpec(memory_space=pltpu.VMEM)
SMEM = pl.BlockSpec(memory_space=pltpu.SMEM)
HBM = pl.BlockSpec(memory_space=pltpu.HBM)


PLANE = ("x", "y", "core")
ALONG_X = [[[(x * 4 + y) * 2 + core for x in range(4)] for y in range(4)] for core in range(2)]
ALONG_Y = [[[(x * 4 + y) * 2 + core for y in range(4)] for x in range(4)] for core in range(2)]
FIRST, SECOND = ALONG_X[0] + ALONG_Y[1], ALONG_Y[0] + ALONG_X[1]


def exchange(a, axes, groups=None):
    return lax.all_to_all(a, axes, split_axis=0, concat_axis=0, axis_index_groups=groups, tiled=True)


def dot(a, b, contract=((1,), (0,))):
    return lax.dot_general(a, b, (contract, ((), ())), preferred_element_type=f32)


def halves(a):
    high = a.astype(bf16)
    return high, (a - high.astype(f32)).astype(bf16)


def dot3(a, b):
    return dot(a[0], b[0]) + (dot(a[0], b[1]) + dot(a[1], b[0]))


def regroup_kernel(place, blocks, pieces):
    def copy(along_x):
        for near in range(4):
            for far in range(4):
                for q in range(4):
                    pieces[near, far, q] = blocks[q, 4 * near + far if along_x else 4 * far + near]

    pl.when(place[0] == 0)(lambda: copy(True))
    pl.when(place[0] != 0)(lambda: copy(False))


def regroup(place, blocks):
    return pl.pallas_call(
        regroup_kernel,
        out_shape=jax.ShapeDtypeStruct((4, 4, 4, 32, 512), bf16),
        in_specs=[SMEM, VMEM],
        out_specs=VMEM,
        compiler_params=pltpu.CompilerParams(vmem_limit_bytes=6 * 2**20),
        name="regroup",
    )(place, blocks)


def first_sum_kernel(arrived, sums):
    for far in range(4):
        for q in range(4):
            total = arrived[0, far, q].astype(f32)
            for source in range(1, 4):
                total = total + arrived[source, far, q].astype(f32)
            sums[far, q] = total.astype(bf16)


def first_sum(arrived):
    return pl.pallas_call(
        first_sum_kernel,
        out_shape=jax.ShapeDtypeStruct((4, 4, 32, 512), bf16),
        in_specs=[VMEM],
        out_specs=VMEM,
        compiler_params=pltpu.CompilerParams(vmem_limit_bytes=4 * 2**20),
        name="first_sum",
    )(arrived)


def second_sum_kernel(arrived, tiles):
    for q in range(4):
        total = arrived[0, q].astype(f32)
        for source in range(1, 4):
            total = total + arrived[source, q].astype(f32)
        for piece in range(16):
            row, column = piece // 4 * 8, piece % 4 * 128
            tiles[piece, q] = total[row : row + 8, column : column + 128].astype(bf16)


def second_sum(arrived):
    return pl.pallas_call(
        second_sum_kernel,
        out_shape=jax.ShapeDtypeStruct((16, 4, 8, 128), bf16),
        in_specs=[VMEM],
        out_specs=VMEM,
        compiler_params=pltpu.CompilerParams(vmem_limit_bytes=4 * 2**20),
        name="second_sum",
    )(arrived)


def ahead_kernel(place, left_stat, right_stat, left_root, right_root, powers, left_base, right_base, right_old):
    start = pl.multiple_of(place[1] * 32, 32)
    for side, root in enumerate((left_root, right_root)):
        first = halves(root[...])
        square = halves(dot3(first, first))
        fourth = halves(dot3(square, square))
        powers[2 * side], powers[2 * side + 1] = halves(dot3(fourth, first))
    kept = dot3(halves(left_stat[...]), (powers[0], powers[1]))
    left_base[...] = (5.0 * left_root[pl.ds(start, 32)] - decay_rate * kept) / 4.0
    kept = dot3(halves(right_stat[...]), (powers[2], powers[3]))
    right_base[...] = (5.0 * right_root[...] - decay_rate * kept) / 4.0
    right_old[...] = decay_rate * right_stat[pl.ds(start, 32)]


def ahead(place, left_stat, right_stat, left_root, right_root):
    shapes = ((4, 512, 512), bf16), ((32, 512), f32), ((512, 512), f32), ((32, 512), f32)
    return pl.pallas_call(
        ahead_kernel,
        out_shape=tuple(jax.ShapeDtypeStruct(*shape) for shape in shapes),
        in_specs=[SMEM] + [VMEM] * 4,
        out_specs=(VMEM,) * 4,
        compiler_params=pltpu.CompilerParams(vmem_limit_bytes=12 * 2**20),
        cost_estimate=pl.CostEstimate(flops=22 * 2 * 512**3, bytes_accessed=6 * 2**20, transcendentals=0),
        name="ahead",
    )(place, left_stat, right_stat, left_root, right_root)


def tail_kernel(
    place, own, left_stat, powers, left_base, right_base, right_old, other_hbm,
    result, left_new, right_new, left_next, right_next, other, grid, full, sem,
):
    copy = pltpu.make_async_copy(other_hbm, other, sem)
    copy.start()
    core, mine = place[0], place[1]
    start = pl.multiple_of(mine * 32, 32)
    gram_weight = (1.0 - decay_rate) / 512
    for tiles, parity in ((own, core), (other, 1 - core)):
        if tiles is other:
            copy.wait()
        for chip in range(8):
            column = pl.multiple_of((chip % 2 * 2 + parity) * 128, 128)
            grid[:, pl.ds(chip // 2 * 8, 8), pl.ds(column, 128)] = tiles[:, chip].astype(f32)
    block = grid[...].reshape(512, 512).astype(bf16)
    rows = grid[mine].astype(bf16)
    gram_rows = gram_weight * dot(rows, block, ((1,), (1,)))
    gram = gram_weight * dot(block, block, ((0,), (0,)))
    full[...] = gram
    left_new[...] = decay_rate * left_stat[...] + gram_rows
    next_rows = left_base[...] - 0.25 * dot3(halves(gram_rows), (powers[0], powers[1]))
    left_next[...] = next_rows
    left_half = dot(next_rows.astype(bf16), block).astype(bf16)
    right_new[...] = right_old[...] + full[pl.ds(start, 32)]
    root = right_base[...] - 0.25 * dot3(halves(gram), (powers[2], powers[3]))
    full[...] = root
    right_next[...] = full[pl.ds(start, 32)]
    result[...] = dot(left_half, root.astype(bf16)).astype(bf16)


def tail(place, *operands):
    rows, whole = (32, 512), (512, 512)
    return pl.pallas_call(
        tail_kernel,
        out_shape=(jax.ShapeDtypeStruct(rows, bf16),) + (jax.ShapeDtypeStruct(rows, f32),) * 4,
        in_specs=[SMEM] + [VMEM] * 6 + [HBM],
        out_specs=(VMEM,) * 5,
        scratch_shapes=[
            pltpu.VMEM((16, 8, 8, 128), bf16), pltpu.VMEM((16, 32, 512), f32), pltpu.VMEM(whole, f32), pltpu.SemaphoreType.DMA,
        ],
        compiler_params=pltpu.CompilerParams(vmem_limit_bytes=12 * 2**20),
        name="tail",
    )(place, *operands)


def held(*arrays):
    return lax.optimization_barrier(arrays)


def per_device(grad_partial, owner_block, left_stat, right_stat, left_root, right_root):
    core = lax.axis_index("core")
    place = jnp.stack([core, lax.axis_index("zl") * 2 + core]).astype(jnp.int32)
    pieces = regroup(place, grad_partial.reshape(4, 16, 32, 512))
    sums = first_sum(exchange(pieces, PLANE, FIRST))
    tiles = second_sum(exchange(sums, PLANE, SECOND))
    by_block, owner_block = held(exchange(tiles, FSDP), owner_block)
    by_slot = jnp.take(by_block.reshape(64, 8, 128), owner_block, axis=0, mode="clip")
    by_slot, *slot = held(by_slot, left_stat[0], right_stat[0], left_root[0], right_root[0])
    parts, *ready = held(exchange(by_slot.reshape(4, 16, 8, 128), "zh"), *ahead(place, *slot))
    mine = parts.astype(f32).sum(0).astype(bf16)
    spread = jnp.broadcast_to(mine[:, None], (16, 8, 8, 128)).reshape(128, 8, 128)
    own = exchange(spread, ("x", "y", "zl")).reshape(16, 8, 8, 128)
    other = lax.ppermute(own, "core", [(0, 1), (1, 0)])
    outs = tail(place, own, left_stat[0], *ready, other)
    return tuple(out[None] for out in outs)


def solution(mesh):
    fine = Mesh(mesh.devices.reshape(4, 4, 4, 8, 2), REP + FSDP)
    in_specs = (
        P(REP, FSDP, None, None),
        P(),
        P(REP, FSDP, None),
        P(REP, None, None),
        P(REP, None, None),
        P(REP, None, None),
    )
    return jax.shard_map(
        per_device, mesh=fine, in_specs=in_specs, out_specs=(P(REP, FSDP, None),) * 5, check_vma=False
    )
```

time: 152 us -> 149 us (0.980)
  blocking collectives: 83.1 us -> 94.6 us
  starting transfers between devices: 31.1 us -> 23.1 us
  waiting for transfers between devices: 19.1 us -> 12.4 us
    all_to_all x3 -> x4, blocking collectives: 83.1 us -> 94.6 us  [exchange(): lax.all_to_all(a, axes, split_axis=0, concat_axis=0, axis_index_groups=gr...]
    all_to_all x1, waiting for transfers between devices: 18.7 us -> 11.2 us  [exchange(): lax.all_to_all(a, axes, split_axis=0, concat_axis=0, axis_index_groups=gr...]
    all_to_all x1, starting transfers between devices: 23.5 us -> 18.4 us  [exchange(): lax.all_to_all(a, axes, split_axis=0, concat_axis=0, axis_index_groups=gr...]
    ppermute x1, starting transfers between devices: 7.61 us -> 4.62 us  [per_device(): other = lax.ppermute(own, 'core', [(0, 1), (1, 0)])]
    pallas_call x3 -> x4, Pallas kernels: 5.62 us -> 7.86 us  [the longest x1 6.85 us: ahead(): pl.pallas_call(ahead_kernel, out_shape=tuple((jax.ShapeDtypeStruct(*shape...]
    unnamed x14 -> x12, local copies, waits for them, and re-layouts: 5.26 us -> 5.27 us
  transfers between devices with their start and end apart: 2 -> 2, of which waited for: 2 -> 2; matrix products, arithmetic and copies ran while one was open for 1% -> 0% of each run, Pallas kernels for 3% -> 5%
where the time goes in v3:
time: 149 us
  blocking collectives  94.6 us (63%)
  starting transfers between devices  23.1 us (16%)
  waiting for transfers between devices  12.4 us (8%)
  Pallas kernels  11.2 us (8%)
  local copies, waits for them, and re-layouts  6.58 us (4%)
    all_to_all x4, blocking collectives, exchange(): lax.all_to_all(a, axes, split_axis=0, concat_axis=0, axis_index_groups=gr...  94.6 us
    all_to_all x1, starting transfers between devices, exchange(): lax.all_to_all(a, axes, split_axis=0, concat_axis=0, axis_index_groups=gr...  18.4 us
    all_to_all x1, waiting for transfers between devices, exchange(): lax.all_to_all(a, axes, split_axis=0, concat_axis=0, axis_index_groups=gr...  11.2 us
    pallas_call x1, Pallas kernels, ahead(): pl.pallas_call(ahead_kernel, out_shape=tuple((jax.ShapeDtypeStruct(*shape...  6.85 us
    unnamed x12, local copies, waits for them, and re-layouts  5.27 us
    ppermute x1, starting transfers between devices, per_device(): other = lax.ppermute(own, 'core', [(0, 1), (1, 0)])  4.62 us
    pallas_call x1, Pallas kernels, tail(): pl.pallas_call(tail_kernel, out_shape=(jax.ShapeDtypeStruct(rows, bf16),)...  3.33 us
  transfers between devices with their start and end apart: 2, of which 2 were waited for; matrix products, arithmetic and copies ran while one was open for 0% of the time, Pallas kernels for 5%

profile of v3, /device:TPU:1, one launch (start us, length us, event | category | flops | bytes accessed | tf_op | source)
XLA Modules:
  0.0 148.6 jit_solution(7463516998555429569)
XLA Ops:
  0.6 0.1 pad_add_fusion.place
  0.7 0.0 copy-start
  0.7 1.6 %copy-done = bf16[1,4,512,512]{3,2,1,0:T(8,128)(2,1)S(1)} copy-done((bf16[1,4,512,512]{3,2,1,0:T(8,128)(2,1)S(1)}, bf16[1,4,512,512]{3,2,1,0:T(8,128)(2,1)}, u32[]{:S(2)}) %copy-start) | copy-done | bytes 2097176
  2.3 0.7 regroup.1
  3.0 20.2 %all_to_all.25.arrived = bf16[4,4,4,32,512]{4,3,2,1,0:T(8,128)(2,1)S(1)} all-to-all(bf16[4,4,4,32,512]{4,3,2,1,0:T(8,128)(2,1)S(1)} %regroup.1), channel_id=1, replica_groups={{0,64,128,192},{16,80,144,208},{32,96,160,224},{48,112,176,240},{1,17,3..., dimensions={0} | all-to-all | bytes 4194304 | tf_op jit(solution)/shard_map/all_to_all | solution.py:24
  23.2 0.0 copy-start.5
  23.2 0.0 copy-start.1
  23.2 0.3 first_sum.1
  23.4 13.7 %all_to_all.26.arrived = bf16[4,4,32,512]{3,2,1,0:T(8,128)(2,1)S(1)} all-to-all(bf16[4,4,32,512]{3,2,1,0:T(8,128)(2,1)S(1)} %first_sum.1), channel_id=1, replica_groups={{0,16,32,48},{64,80,96,112},{128,144,160,176},{192,208,224,240},{1,65,1..., dimensions={0} | all-to-all | bytes 1048576 | tf_op jit(solution)/shard_map/all_to_all | solution.py:24
  37.1 0.1 second_sum.1
  37.2 27.1 %all_to_all.27 = bf16[16,4,8,128]{3,2,1,0:T(8,128)(2,1)S(1)} all-to-all(bf16[16,4,8,128]{3,2,1,0:T(8,128)(2,1)S(1)} %second_sum.1), channel_id=1, replica_groups=mesh['zh'=4,'x'=4,'y'=4,'zl'=8,'core'=2] {'zl','core'}, dimensions={0} | all-to-all | bytes 262144 | tf_op jit(solution)/shard_map/all_to_all | solution.py:24
  64.3 0.0 copy-done.5
  64.3 1.3 gather_fusion
  65.5 18.4 %all-to-all-start.3 = ((bf16[4,16,8,128]{3,2,1,0:T(8,128)(2,1)}), bf16[4,16,8,128]{3,2,1,0:T(8,128)(2,1)S(1)}, u32[]{:S(2)}, u32[]{:S(2)}) async-start(bf16[4,16,8,128]{3,2,1,0:T(8,128)(2,1)} %bitcast.8), calls=%async_computation.3 | async-start | bytes 262144 | tf_op jit(solution)/shard_map/all_to_all | solution.py:24
  84.0 0.0 copy-done.1
  84.0 0.0 copy-start.2
  84.0 1.2 copy-done.2
  85.2 0.0 copy-start.3
  85.2 1.2 copy-done.3
  86.4 0.0 copy-start.4
  86.4 1.2 copy-done.4
  87.7 6.8 %ahead.1 = (bf16[4,512,512]{2,1,0:T(8,128)(2,1)S(1)}, f32[32,512]{1,0:T(8,128)S(1)}, f32[512,512]{1,0:T(8,128)S(1)}, f32[32,512]{1,0:T(8,128)S(1)}) custom-call(s32[2]{0:T(128)S(1)} %pad_add_fusion.place, f32[32,512]{1,0:T(8,128)S(1)} %bitcast.19, f32[512,512]{1,0:T(8,128)S(1)} %bitcast.21, f32[512,512]{1,0:T(8,128)S(1)} %bitcast.22, f32[512,512]{1,0:T(8,128)S(1)} %bitcast.23), custom_call_target="tpu_custom_call" | custom-call | flops 5905580032 | bytes 6291456 | tf_op jit(solution)/shard_map/ahead/pallas_call | solution.py:119
  94.5 11.2 %all-to-all-done.3 = bf16[4,16,8,128]{3,2,1,0:T(8,128)(2,1)S(1)} async-done(((bf16[4,16,8,128]{3,2,1,0:T(8,128)(2,1)}), bf16[4,16,8,128]{3,2,1,0:T(8,128)(2,1)S(1)}, u32[]{:S(2)}, u32[]{:S(2)}) %all-to-all-start.3) | async-done | bytes 131104 | tf_op jit(solution)/shard_map/all_to_all | solution.py:24
  105.8 33.7 %all_to_all.28 = bf16[128,8,128]{2,1,0:T(8,128)(2,1)S(1)} all-to-all(bf16[128,8,128]{2,1,0:T(8,128)(2,1)S(1)} %bitcast.24), channel_id=1, replica_groups=mesh['zh'=4,'x'=4,'y'=4,'zl'=8,'core'=2] {'x','y','zl'}, dimensions={0} | all-to-all | bytes 524288 | tf_op jit(solution)/shard_map/all_to_all | solution.py:24
  139.5 4.6 %collective-permute-start = (bf16[16,8,8,128]{3,2,1,0:T(8,128)(2,1)S(1)}, bf16[16,8,8,128]{3,2,1,0:T(8,128)(2,1)S(1)}, u32[]{:S(2)}, u32[]{:S(2)}) collective-permute-start(bf16[16,8,8,128]{3,2,1,0:T(8,128)(2,1)S(1)} %bitcast.17), channel_id=1, source_target_pairs={{0,1},{1,0},{2,3},{3,2},{4,5},{5,4},{6,7},{7,6},{8,9},{9,8},{10,11... | collective-permute-start | bytes 786440 | tf_op jit(solution)/shard_map/ppermute | solution.py:193
  144.1 1.1 collective-permute-done.other_hbm
  145.3 3.3 %tail.1 = (bf16[32,512]{1,0:T(8,128)(2,1)}, f32[32,512]{1,0:T(8,128)}, f32[32,512]{1,0:T(8,128)}, f32[32,512]{1,0:T(8,128)}, f32[32,512]{1,0:T(8,128)}) custom-call(s32[2]{0:T(128)S(1)} %pad_add_fusion.place, bf16[16,8,8,128]{3,2,1,0:T(8,128)(2,1)S(1)} %bitcast.18, f32[32,512]{1,0:T(8,128)S(1)} %bitcast.20, ...), custom_call_target="tpu_custom_call" | custom-call | tf_op jit(solution)/shard_map/tail/pallas_call | solution.py:163
  (3 shorter events, 0.1 us)
Async XLA Ops:
  0.7 1.6 %copy-start = (bf16[1,4,512,512]{3,2,1,0:T(8,128)(2,1)S(1)}, bf16[1,4,512,512]{3,2,1,0:T(8,128)(2,1)}, u32[]{:S(2)}) copy-start(bf16[1,4,512,512]{3,2,1,0:T(8,128)(2,1)} %param.6) | copy-start | bytes 6291460
  23.2 41.1 %copy-start.5 = (s32[64]{0:T(128)S(1)}, s32[64]{0:T(128)}, u32[]{:S(2)}) copy-start(s32[64]{0:T(128)} %param.7) | copy-start | bytes 772
  23.2 60.8 %copy-start.1 = (f32[1,32,512]{2,1,0:T(8,128)S(1)}, f32[1,32,512]{2,1,0:T(8,128)}, u32[]{:S(2)}) copy-start(f32[1,32,512]{2,1,0:T(8,128)} %param.8) | copy-start | bytes 196612
  65.5 40.2 %all-to-all-start.3 = ((bf16[4,16,8,128]{3,2,1,0:T(8,128)(2,1)}), bf16[4,16,8,128]{3,2,1,0:T(8,128)(2,1)S(1)}, u32[]{:S(2)}, u32[]{:S(2)}) async-start(bf16[4,16,8,128]{3,2,1,0:T(8,128)(2,1)} %bitcast.8), calls=%async_computation.3 | async-start | bytes 262144 | tf_op jit(solution)/shard_map/all_to_all | solution.py:24
  84.0 1.2 copy-start.2
  85.2 1.2 copy-start.3
  86.4 1.2 copy-start.4
  139.5 5.8 %collective-permute-start = (bf16[16,8,8,128]{3,2,1,0:T(8,128)(2,1)S(1)}, bf16[16,8,8,128]{3,2,1,0:T(8,128)(2,1)S(1)}, u32[]{:S(2)}, u32[]{:S(2)}) collective-permute-start(bf16[16,8,8,128]{3,2,1,0:T(8,128)(2,1)S(1)} %bitcast.17), channel_id=1, source_target_pairs={{0,1},{1,0},{2,3},{3,2},{4,5},{5,4},{6,7},{7,6},{8,9},{9,8},{10,11... | collective-permute-start | bytes 786440 | tf_op jit(solution)/shard_map/ppermute | solution.py:193

commit v4 on v3

--- a/solution.py
+++ b/solution.py
@@ -15,9 +15,18 @@
 
 
 PLANE = ("x", "y", "core")
-ALONG_X = [[[(x * 4 + y) * 2 + core for x in range(4)] for y in range(4)] for core in range(2)]
-ALONG_Y = [[[(x * 4 + y) * 2 + core for y in range(4)] for x in range(4)] for core in range(2)]
-FIRST, SECOND = ALONG_X[0] + ALONG_Y[1], ALONG_Y[0] + ALONG_X[1]
+EVEN, ODD = ((0, 1), (2, 3)), ((1, 2), (3, 0))
+PLACES = (((0, 1, 1, 0), (1, 0, 1, 0)), ((0, 0, 1, 1), (0, 1, 0, 1)))
+
+
+def squares(pairs, places, core):
+    chips = [[(x, y) for x in xs for y in ys] for xs in pairs for ys in pairs]
+    ordered = [sorted(square, key=lambda chip: 2 * places[chip[0]] + places[chip[1]]) for square in chips]
+    return [[(x * 4 + y) * 2 + core for x, y in square] for square in ordered]
+
+
+FIRST = squares(EVEN, PLACES[0][0], 0) + squares(ODD, PLACES[1][0], 1)
+SECOND = squares(ODD, PLACES[0][1], 0) + squares(EVEN, PLACES[1][1], 1)
 
 
 def exchange(a, axes, groups=None):
@@ -38,14 +47,15 @@
 
 
 def regroup_kernel(place, blocks, pieces):
-    def copy(along_x):
-        for near in range(4):
-            for far in range(4):
+    def copy(first, second):
+        for x in range(4):
+            for y in range(4):
+                near, far = 2 * first[x] + first[y], 2 * second[x] + second[y]
                 for q in range(4):
-                    pieces[near, far, q] = blocks[q, 4 * near + far if along_x else 4 * far + near]
-
-    pl.when(place[0] == 0)(lambda: copy(True))
-    pl.when(place[0] != 0)(lambda: copy(False))
+                    pieces[near, far, q] = blocks[q, 4 * x + y]
+
+    pl.when(place[0] == 0)(lambda: copy(*PLACES[0]))
+    pl.when(place[0] != 0)(lambda: copy(*PLACES[1]))
 
 
 def regroup(place, blocks):

time: 149 us -> 150 us (level)
  blocking collectives: 94.6 us -> 96.2 us
    all_to_all x4, blocking collectives: 94.6 us -> 96.2 us  [exchange(): lax.all_to_all(a, axes, split_axis=0, concat_axis=0, axis_index_groups=gr...]
where the time goes in v4:
time: 150 us; the launch traced here: 149 us
  blocking collectives  96.2 us (64%)
  starting transfers between devices  21.9 us (15%)
  waiting for transfers between devices  12.4 us (8%)
  Pallas kernels  11.2 us (7%)
  local copies, waits for them, and re-layouts  6.58 us (4%)
    all_to_all x4, blocking collectives, exchange(): lax.all_to_all(a, axes, split_axis=0, concat_axis=0, axis_index_groups=gr...  96.2 us
    all_to_all x1, starting transfers between devices, exchange(): lax.all_to_all(a, axes, split_axis=0, concat_axis=0, axis_index_groups=gr...  17.3 us
    all_to_all x1, waiting for transfers between devices, exchange(): lax.all_to_all(a, axes, split_axis=0, concat_axis=0, axis_index_groups=gr...  11.2 us
    pallas_call x1, Pallas kernels, ahead(): pl.pallas_call(ahead_kernel, out_shape=tuple((jax.ShapeDtypeStruct(*shape...  6.85 us
    unnamed x12, local copies, waits for them, and re-layouts  5.27 us
    ppermute x1, starting transfers between devices, per_device(): other = lax.ppermute(own, 'core', [(0, 1), (1, 0)])  4.62 us
    pallas_call x1, Pallas kernels, tail(): pl.pallas_call(tail_kernel, out_shape=(jax.ShapeDtypeStruct(rows, bf16),)...  3.32 us
  transfers between devices with their start and end apart: 2, of which 2 were waited for; matrix products, arithmetic and copies ran while one was open for 0% of the time, Pallas kernels for 5%

profile of v4, /device:TPU:1, one launch (start us, length us, event | category | flops | bytes accessed | tf_op | source)
XLA Modules:
  0.0 149.1 jit_solution(6174065148641840629)
XLA Ops:
  0.6 0.1 pad_add_fusion.place
  0.7 0.0 copy-start
  0.7 1.6 %copy-done = bf16[1,4,512,512]{3,2,1,0:T(8,128)(2,1)S(1)} copy-done((bf16[1,4,512,512]{3,2,1,0:T(8,128)(2,1)S(1)}, bf16[1,4,512,512]{3,2,1,0:T(8,128)(2,1)}, u32[]{:S(2)}) %copy-start) | copy-done | bytes 2097176
  2.3 0.7 regroup.1
  3.0 23.7 %all_to_all.25.arrived = bf16[4,4,4,32,512]{4,3,2,1,0:T(8,128)(2,1)S(1)} all-to-all(bf16[4,4,4,32,512]{4,3,2,1,0:T(8,128)(2,1)S(1)} %regroup.1), channel_id=1, replica_groups={{0,16,64,80},{48,32,112,96},{192,208,128,144},{240,224,176,160},{81,97,..., dimensions={0} | all-to-all | bytes 4194304 | tf_op jit(solution)/shard_map/all_to_all | solution.py:33
  26.7 0.0 copy-start.5
  26.7 0.0 copy-start.1
  26.7 0.3 first_sum.1
  26.9 10.4 %all_to_all.26.arrived = bf16[4,4,32,512]{3,2,1,0:T(8,128)(2,1)S(1)} all-to-all(bf16[4,4,32,512]{3,2,1,0:T(8,128)(2,1)S(1)} %first_sum.1), channel_id=1, replica_groups={{80,96,144,160},{112,64,176,128},{208,224,16,32},{240,192,48,0},{1,17,6..., dimensions={0} | all-to-all | bytes 1048576 | tf_op jit(solution)/shard_map/all_to_all | solution.py:33
  37.3 0.1 second_sum.1
  37.4 25.8 %all_to_all.27 = bf16[16,4,8,128]{3,2,1,0:T(8,128)(2,1)S(1)} all-to-all(bf16[16,4,8,128]{3,2,1,0:T(8,128)(2,1)S(1)} %second_sum.1), channel_id=1, replica_groups=mesh['zh'=4,'x'=4,'y'=4,'zl'=8,'core'=2] {'zl','core'}, dimensions={0} | all-to-all | bytes 262144 | tf_op jit(solution)/shard_map/all_to_all | solution.py:33
  63.2 0.0 copy-done.5
  63.2 1.3 gather_fusion
  64.4 17.3 %all-to-all-start.3 = ((bf16[4,16,8,128]{3,2,1,0:T(8,128)(2,1)}), bf16[4,16,8,128]{3,2,1,0:T(8,128)(2,1)S(1)}, u32[]{:S(2)}, u32[]{:S(2)}) async-start(bf16[4,16,8,128]{3,2,1,0:T(8,128)(2,1)} %bitcast.8), calls=%async_computation.3 | async-start | bytes 262144 | tf_op jit(solution)/shard_map/all_to_all | solution.py:33
  81.8 0.0 copy-done.1
  81.8 0.0 copy-start.2
  81.8 1.2 copy-done.2
  83.0 0.0 copy-start.3
  83.0 1.2 copy-done.3
  84.2 0.0 copy-start.4
  84.2 1.2 copy-done.4
  85.5 6.8 %ahead.1 = (bf16[4,512,512]{2,1,0:T(8,128)(2,1)S(1)}, f32[32,512]{1,0:T(8,128)S(1)}, f32[512,512]{1,0:T(8,128)S(1)}, f32[32,512]{1,0:T(8,128)S(1)}) custom-call(s32[2]{0:T(128)S(1)} %pad_add_fusion.place, f32[32,512]{1,0:T(8,128)S(1)} %bitcast.19, f32[512,512]{1,0:T(8,128)S(1)} %bitcast.21, f32[512,512]{1,0:T(8,128)S(1)} %bitcast.22, f32[512,512]{1,0:T(8,128)S(1)} %bitcast.23), custom_call_target="tpu_custom_call" | custom-call | flops 5905580032 | bytes 6291456 | tf_op jit(solution)/shard_map/ahead/pallas_call | solution.py:129
  92.3 11.2 %all-to-all-done.3 = bf16[4,16,8,128]{3,2,1,0:T(8,128)(2,1)S(1)} async-done(((bf16[4,16,8,128]{3,2,1,0:T(8,128)(2,1)}), bf16[4,16,8,128]{3,2,1,0:T(8,128)(2,1)S(1)}, u32[]{:S(2)}, u32[]{:S(2)}) %all-to-all-start.3) | async-done | bytes 131104 | tf_op jit(solution)/shard_map/all_to_all | solution.py:33
  103.6 36.4 %all_to_all.28 = bf16[128,8,128]{2,1,0:T(8,128)(2,1)S(1)} all-to-all(bf16[128,8,128]{2,1,0:T(8,128)(2,1)S(1)} %bitcast.24), channel_id=1, replica_groups=mesh['zh'=4,'x'=4,'y'=4,'zl'=8,'core'=2] {'x','y','zl'}, dimensions={0} | all-to-all | bytes 524288 | tf_op jit(solution)/shard_map/all_to_all | solution.py:33
  140.0 4.6 %collective-permute-start = (bf16[16,8,8,128]{3,2,1,0:T(8,128)(2,1)S(1)}, bf16[16,8,8,128]{3,2,1,0:T(8,128)(2,1)S(1)}, u32[]{:S(2)}, u32[]{:S(2)}) collective-permute-start(bf16[16,8,8,128]{3,2,1,0:T(8,128)(2,1)S(1)} %bitcast.17), channel_id=1, source_target_pairs={{0,1},{1,0},{2,3},{3,2},{4,5},{5,4},{6,7},{7,6},{8,9},{9,8},{10,11... | collective-permute-start | bytes 786440 | tf_op jit(solution)/shard_map/ppermute | solution.py:203
  144.6 1.1 collective-permute-done.other_hbm
  145.7 3.3 %tail.1 = (bf16[32,512]{1,0:T(8,128)(2,1)}, f32[32,512]{1,0:T(8,128)}, f32[32,512]{1,0:T(8,128)}, f32[32,512]{1,0:T(8,128)}, f32[32,512]{1,0:T(8,128)}) custom-call(s32[2]{0:T(128)S(1)} %pad_add_fusion.place, bf16[16,8,8,128]{3,2,1,0:T(8,128)(2,1)S(1)} %bitcast.18, f32[32,512]{1,0:T(8,128)S(1)} %bitcast.20, ...), custom_call_target="tpu_custom_call" | custom-call | tf_op jit(solution)/shard_map/tail/pallas_call | solution.py:173
  (3 shorter events, 0.1 us)
Async XLA Ops:
  0.7 1.6 %copy-start = (bf16[1,4,512,512]{3,2,1,0:T(8,128)(2,1)S(1)}, bf16[1,4,512,512]{3,2,1,0:T(8,128)(2,1)}, u32[]{:S(2)}) copy-start(bf16[1,4,512,512]{3,2,1,0:T(8,128)(2,1)} %param.6) | copy-start | bytes 6291460
  26.7 36.5 %copy-start.5 = (s32[64]{0:T(128)S(1)}, s32[64]{0:T(128)}, u32[]{:S(2)}) copy-start(s32[64]{0:T(128)} %param.7) | copy-start | bytes 772
  26.7 55.1 %copy-start.1 = (f32[1,32,512]{2,1,0:T(8,128)S(1)}, f32[1,32,512]{2,1,0:T(8,128)}, u32[]{:S(2)}) copy-start(f32[1,32,512]{2,1,0:T(8,128)} %param.8) | copy-start | bytes 196612
  64.4 39.1 %all-to-all-start.3 = ((bf16[4,16,8,128]{3,2,1,0:T(8,128)(2,1)}), bf16[4,16,8,128]{3,2,1,0:T(8,128)(2,1)S(1)}, u32[]{:S(2)}, u32[]{:S(2)}) async-start(bf16[4,16,8,128]{3,2,1,0:T(8,128)(2,1)} %bitcast.8), calls=%async_computation.3 | async-start | bytes 262144 | tf_op jit(solution)/shard_map/all_to_all | solution.py:33
  81.8 1.2 copy-start.2
  83.0 1.2 copy-start.3
  84.2 1.2 copy-start.4
  140.0 5.8 %collective-permute-start = (bf16[16,8,8,128]{3,2,1,0:T(8,128)(2,1)S(1)}, bf16[16,8,8,128]{3,2,1,0:T(8,128)(2,1)S(1)}, u32[]{:S(2)}, u32[]{:S(2)}) collective-permute-start(bf16[16,8,8,128]{3,2,1,0:T(8,128)(2,1)S(1)} %bitcast.17), channel_id=1, source_target_pairs={{0,1},{1,0},{2,3},{3,2},{4,5},{5,4},{6,7},{7,6},{8,9},{9,8},{10,11... | collective-permute-start | bytes 786440 | tf_op jit(solution)/shard_map/ppermute | solution.py:203
